TPU v7x, 128 devices: a whole 4x4x4 slice. The times are simulated.
128 devices in a mesh: grp: 4 (over y), shard: 32 (over x, z, core).
Axes of the slice: x: 4, y: 4, z: 4, core: 2. Of those that a mesh axis runs over, the one named last changes fastest.
Arguments:
- new_rows: bfloat16 [32768, 1024], P(('grp', 'shard'))
- cluster_ids: int32 [32768], P(('grp', 'shard')), may hold values from 0 to 7, as said below
- new_order: int32 [32768], P(('grp', 'shard')), may hold values from 0 to 2147483646
- codes: bfloat16 [8, 8192, 1024], P('grp', 'shard'), may hold values from -8 to 8
- scales: float32 [8, 1024], P('grp')
- offsets: float32 [8, 1024], P('grp')
- counts: int32 [8], P('grp'), may hold values from 1024 to 8192, as said below
- earlier_order: int32 [8, 8192], P('grp', 'shard'), may hold values from 1 to 2147483646
Outputs:
- max_similarity: float32 [32768], P(('grp', 'shard'))
Inputs may be any that keep to these rules, and one draw needn't show every extreme that they name: `cluster_ids`: in each device's block of 256 rows, no group's clusters are named by more than 128 rows, and some group's clusters are named by exactly 128 rows. `counts`: some cluster has all 8192 slots live.
All inputs are finite; a program needn't handle non-finite values.
Results may differ from a plain program's by a relative error of at most 0.00047.
Values may be sent and summed in bfloat16 or wider, within the bound.
A program may use at most 128 MiB of HBM per device.

v0:
```python
import jax
import jax.numpy as jnp
from jax import lax
from jax.sharding import PartitionSpec as P

epsilon = 1e-06


def unit_rows(values):
    return (values / jnp.sqrt(jnp.sum(values * values, axis=-1, keepdims=True) + epsilon)).astype(
        jnp.bfloat16
    )


def score_clusters(
    running, queries, query_cluster, query_order, key_source, key_order, live_counts, prepare
):
    width = key_source.shape[1]
    positions = jnp.arange(width, dtype=jnp.int32)
    best = running
    for cluster in range(key_source.shape[0]):
        cluster_keys = prepare(key_source[cluster], cluster)
        scores = jnp.dot(queries, cluster_keys.T, preferred_element_type=jnp.float32)
        allowed = (
            (query_cluster[:, None] == cluster)
            & (positions[None, :] < live_counts[cluster])
            & (key_order[cluster][None, :] < query_order[:, None])
        )
        best = jnp.maximum(best, jnp.max(jnp.where(allowed, scores, -1.0), axis=1))
    return best


def per_device(new_rows, cluster_ids, new_order, codes, scales, offsets, counts, earlier_order):
    groups = lax.axis_size("grp")
    owned_count = codes.shape[0]
    local_rows = new_rows.shape[0]
    capacity = local_rows // 2
    queries = unit_rows(new_rows.astype(jnp.float32))
    target = cluster_ids // owned_count
    onehot = (target[:, None] == jnp.arange(groups, dtype=jnp.int32)[None, :]).astype(jnp.int32)
    slot_rank = jnp.sum((jnp.cumsum(onehot, axis=0) - onehot) * onehot, axis=1)
    position = target * capacity + slot_rank
    received = groups * capacity
    matches = position[None, :] == jnp.arange(received, dtype=jnp.int32)[:, None]
    filled = jnp.any(matches, axis=1)
    source_row = jnp.sum(
        jnp.where(matches, jnp.arange(local_rows, dtype=jnp.int32)[None, :], 0), axis=1
    )
    send_rows = jnp.take(queries, source_row, axis=0).reshape(groups, capacity, queries.shape[1])
    send_cluster = jnp.where(filled, jnp.take(cluster_ids % owned_count, source_row), 0).reshape(
        groups, capacity
    )
    send_order = jnp.where(filled, jnp.take(new_order, source_row), 0).reshape(groups, capacity)
    got_rows, got_cluster, got_order = (
        lax.all_to_all(send_rows, "grp", split_axis=0, concat_axis=0, tiled=True),
        lax.all_to_all(send_cluster, "grp", split_axis=0, concat_axis=0, tiled=True),
        lax.all_to_all(send_order, "grp", split_axis=0, concat_axis=0, tiled=True),
    )
    got_rows = got_rows.reshape(received, queries.shape[1])
    got_cluster = got_cluster.reshape(received)
    got_order = got_order.reshape(received)
    starting = jnp.zeros((received,), jnp.float32)

    def decode_one(code_rows, cluster):
        return unit_rows(
            code_rows.astype(jnp.float32) * scales[cluster][None, :] + offsets[cluster][None, :]
        )

    top_score = score_clusters(
        starting,
        got_rows,
        got_cluster,
        got_order,
        lax.all_gather(codes, "shard", axis=1, tiled=True),
        lax.all_gather(earlier_order, "shard", axis=1, tiled=True),
        counts,
        decode_one,
    )
    answered = lax.all_to_all(
        top_score.reshape(groups, capacity), "grp", split_axis=0, concat_axis=0, tiled=True
    )
    return jnp.take(answered.reshape(received), position)


def solution(mesh):
    return jax.shard_map(
        per_device,
        mesh=mesh,
        in_specs=(
            P(("grp", "shard"), None),
            P(("grp", "shard")),
            P(("grp", "shard")),
            P("grp", "shard", None),
            P("grp", None),
            P("grp", None),
            P("grp"),
            P("grp", "shard"),
        ),
        out_specs=P(("grp", "shard")),
        check_vma=False,
    )
```

profile of v0, /device:TPU:0, one launch (start us, length us, event | category | flops | bytes accessed | tf_op | source)
XLA Modules:
  0.0 194.7 jit_solution(17353483784496994221)
XLA Ops:
  6.5 0.7 all-gather.2.cloned.1.call-update
  7.3 0.7 and_select_fusion
  8.0 1.2 reduce-window.6
  9.6 0.6 compare_select_fusion.3
  10.2 0.1 select_reduce_fusion.2
  10.3 3.5 %gather_fusion.2 = s32[512]{0:T(512)S(1)} fusion(s32[256]{0:T(256)S(1)} %get-tuple-element.20, s32[1024]{0:T(1024)S(1)} %pad_clamp_fusion.2), kind=kCustom, calls=%fused_computation.clone | custom fusion | bytes 6144 | tf_op jit(solution)/shard_map/jit(_take)/gather | solution.py:50
  13.9 3.5 %gather_fusion.3 = s32[512]{0:T(512)S(1)} fusion(s32[256]{0:T(256)S(1)} %copy-done, s32[1024]{0:T(1024)S(1)} %pad_clamp_fusion.2), kind=kCustom, calls=%fused_computation.1.clone | custom fusion | bytes 6144 | tf_op jit(solution)/shard_map/jit(_take)/gather | solution.py:53
  17.4 0.2 fusion.28
  17.6 0.5 select_select_fusion.1
  18.1 4.5 %all-to-all-start = ((s32[4,1,128]{2,1,0:T(1,128)}), s32[4,1,128]{2,1,0:T(1,128)S(1)}, u32[]{:S(2)}, u32[]{:S(2)}) async-start(s32[4,1,128]{2,1,0:T(1,128)} %bitcast.3), calls=%async_computation | async-start | bytes 4096 | tf_op jit(solution)/shard_map/all_to_all | solution.py:56
  22.7 1.3 fusion.26
  24.0 1.4 fusion.27
  25.3 2.1 %gather_fusion = bf16[512,1024]{1,0:T(8,128)(2,1)S(1)} fusion(bf16[256,1024]{1,0:T(8,128)(2,1)S(1)} %fusion.27, s32[1024]{0:T(1024)S(1)} %pad_clamp_fusion.1), kind=kCustom, calls=%fused_computation.2 | custom fusion | bytes 2099200 | tf_op jit(solution)/shard_map/jit(_take)/gather | solution.py:49
  27.4 25.5 %all_gather.6 = s32[2,8192]{1,0:T(2,128)S(1)} all-gather(s32[2,256]{1,0:T(2,128)} %param.17), channel_id=1, replica_groups=mesh['grp'=4,'shard'=32] {'shard'}, dimensions={1}, use_global_device_ids=true | all-gather | bytes 67584 | tf_op jit(solution)/shard_map/all_gather | solution.py:75
  52.9 1.3 fusion.35
  54.2 0.7 iota_compare_fusion.2
  54.9 0.8 fusion.33
  55.7 0.8 fusion.34
  56.5 1.2 broadcast_select_fusion
  57.7 0.6 iota_compare_fusion.1
  58.2 4.7 %all-to-all-start.1 = ((s32[4,1,128]{2,1,0:T(1,128)}), s32[4,1,128]{2,1,0:T(1,128)S(1)}, u32[]{:S(2)}, u32[]{:S(2)}) async-start(s32[4,1,128]{2,1,0:T(1,128)} %bitcast.6), calls=%async_computation.1 | async-start | bytes 4096 | tf_op jit(solution)/shard_map/all_to_all | solution.py:57
  63.0 5.2 %all-to-all-done.1 = s32[4,1,128]{2,1,0:T(1,128)S(1)} async-done(((s32[4,1,128]{2,1,0:T(1,128)}), s32[4,1,128]{2,1,0:T(1,128)S(1)}, u32[]{:S(2)}, u32[]{:S(2)}) %all-to-all-start.1) | async-done | bytes 2080 | tf_op jit(solution)/shard_map/all_to_all | solution.py:57
  68.2 3.5 %all-to-all-start.2 = ((bf16[4,128,1024]{2,1,0:T(8,128)(2,1)}), bf16[4,128,1024]{2,1,0:T(8,128)(2,1)S(1)}, u32[]{:S(2)}, u32[]{:S(2)}) async-start(bf16[4,128,1024]{2,1,0:T(8,128)(2,1)} %broadcast_select_fusion), calls=%async_computation.2 | async-start | bytes 2097152 | tf_op jit(solution)/shard_map/all_to_all | solution.py:55
  71.8 54.4 %all-gather.2.cloned.1.call-done = bf16[2,8192,1024]{2,1,0:T(8,128)(2,1)} async-done(((bf16[2,256,1024]{2,1,0:T(8,128)(2,1)}), bf16[2,8192,1024]{2,1,0:T(8,128)(2,1)}) %all-gather.2.cloned.1.call-update) | async-done | bytes 33554448 | tf_op jit(solution)/shard_map/all_gather | solution.py:74
  126.2 20.2 %fusion.6 = (f32[8192]{0:T(1024)S(1)}, f32[8192]{0:T(1024)S(1)}) fusion(f32[1024]{0:T(1024)S(1)} %bitcast.89, f32[1024]{0:T(1024)S(1)} %bitcast.87, bf16[2,8192,1024]{2,1,0:T(8,128)(2,1)} %all-gather.2.cloned.1.call-done, f32[1024]{0:T(1024)S(1)} %bitcast.85, f32[1024]{0:T(1024)S(1)} %bitcast.83), kind=kLoop, calls=%fused_computation.14 | loop fusion | flops 83869696 | bytes 33636352 | tf_op jit(solution)/shard_map/reduce_sum | solution.py:10
  146.4 14.4 %select_reduce_fusion.1 = f32[512]{0:T(512)S(1)} fusion(s32[8192]{0:T(1024)S(1)} %bitcast.81, s32[512]{0:T(512)S(1)} %bitcast.93, pred[8192]{0:T(1024)(128)(4,1)S(1)} %iota_compare_fusion.2, pred[512]{0:T(512)(128)(4,1)S(1)} %bitcast.96, bf16[512,1024]{1,0:T(8,128)(2,1)S(1)} %bitcast.77, f32[8192]{0:T(1024)S(1)} %get-tuple-element.25, ...), kind=kOutput, calls=%fused_computation.25 | convolution fusion | flops 8652849152 | bytes 17912320 | tf_op jit(solution)/shard_map/dot_general | solution.py:23
  160.9 14.5 %select_reduce_fusion = f32[512]{0:T(512)S(1)} fusion(s32[8192]{0:T(1024)S(1)} %bitcast.80, s32[512]{0:T(512)S(1)} %bitcast.94, pred[8192]{0:T(1024)(128)(4,1)S(1)} %iota_compare_fusion.1, pred[512]{0:T(512)(128)(4,1)S(1)} %bitcast.95, bf16[512,1024]{1,0:T(8,128)(2,1)S(1)} %bitcast.78, f32[8192]{0:T(1024)S(1)} %get-tuple-element.24, f32[1024]{0:T(1024)S(1)} %bitcast.86, ...), kind=kOutput, calls=%fused_computation.24 | convolution fusion | flops 8652849152 | bytes 17912320 | tf_op jit(solution)/shard_map/dot_general | solution.py:23
  175.3 0.6 maximum_maximum_fusion
  175.9 4.3 %all-to-all-start.3 = ((f32[4,1,128]{2,1,0:T(1,128)}), f32[4,1,128]{2,1,0:T(1,128)S(1)}, u32[]{:S(2)}, u32[]{:S(2)}) async-start(f32[4,1,128]{2,1,0:T(1,128)} %bitcast.23), calls=%async_computation.3 | async-start | bytes 4096 | tf_op jit(solution)/shard_map/all_to_all | solution.py:79
  180.2 5.1 %all-to-all-done.3 = f32[4,1,128]{2,1,0:T(1,128)S(1)} async-done(((f32[4,1,128]{2,1,0:T(1,128)}), f32[4,1,128]{2,1,0:T(1,128)S(1)}, u32[]{:S(2)}, u32[]{:S(2)}) %all-to-all-start.3) | async-done | bytes 2080 | tf_op jit(solution)/shard_map/all_to_all | solution.py:79
  185.3 1.9 gather_fusion.1
  187.3 0.6 and_select_fusion.1
  (29 shorter events, 0.6 us)
Async XLA Ops:
  6.5 7.3 %copy-start = (s32[256]{0:T(256)S(1)}, s32[256]{0:T(256)}, u32[]{:S(2)}) copy-start(s32[256]{0:T(256)} %param.12) | copy-start | bytes 3076
  6.5 119.7 %all-gather.2.cloned.1.call-start = ((), (), s32[]{:S(2)}) async-start(), calls=%async_computation.4 | async-start | bytes 34603008 | tf_op jit(solution)/shard_map/all_gather | solution.py:74
  10.2 13.8 %copy-start.1 = (s32[256]{0:T(256)}, s32[256]{0:T(256)S(1)}, u32[]{:S(2)}) copy-start(s32[256]{0:T(256)S(1)} %get-tuple-element.11) | copy-start | bytes 3076
  18.1 40.1 %all-to-all-start = ((s32[4,1,128]{2,1,0:T(1,128)}), s32[4,1,128]{2,1,0:T(1,128)S(1)}, u32[]{:S(2)}, u32[]{:S(2)}) async-start(s32[4,1,128]{2,1,0:T(1,128)} %bitcast.3), calls=%async_computation | async-start | bytes 4096 | tf_op jit(solution)/shard_map/all_to_all | solution.py:56
  58.2 10.0 %all-to-all-start.1 = ((s32[4,1,128]{2,1,0:T(1,128)}), s32[4,1,128]{2,1,0:T(1,128)S(1)}, u32[]{:S(2)}, u32[]{:S(2)}) async-start(s32[4,1,128]{2,1,0:T(1,128)} %bitcast.6), calls=%async_computation.1 | async-start | bytes 4096 | tf_op jit(solution)/shard_map/all_to_all | solution.py:57
  68.2 78.2 %all-to-all-start.2 = ((bf16[4,128,1024]{2,1,0:T(8,128)(2,1)}), bf16[4,128,1024]{2,1,0:T(8,128)(2,1)S(1)}, u32[]{:S(2)}, u32[]{:S(2)}) async-start(bf16[4,128,1024]{2,1,0:T(8,128)(2,1)} %broadcast_select_fusion), calls=%async_computation.2 | async-start | bytes 2097152 | tf_op jit(solution)/shard_map/all_to_all | solution.py:55
  160.8 19.4 %copy-start.3 = (s32[256]{0:T(256)S(1)}, s32[256]{0:T(256)}, u32[]{:S(2)}) copy-start(s32[256]{0:T(256)} %get-tuple-element.10) | copy-start | bytes 3076
  160.8 26.4 %copy-start.2 = (s32[256]{0:T(256)S(1)}, s32[256]{0:T(256)}, u32[]{:S(2)}) copy-start(s32[256]{0:T(256)} %copy-done.1) | copy-start | bytes 3076
  175.9 9.4 %all-to-all-start.3 = ((f32[4,1,128]{2,1,0:T(1,128)}), f32[4,1,128]{2,1,0:T(1,128)S(1)}, u32[]{:S(2)}, u32[]{:S(2)}) async-start(f32[4,1,128]{2,1,0:T(1,128)} %bitcast.23), calls=%async_computation.3 | async-start | bytes 4096 | tf_op jit(solution)/shard_map/all_to_all | solution.py:79
Sparse Core Ops, SparseCore 0:
  9.7 116.4 all-gather.1
where the time goes:
time: 195 us
  waiting for transfers between devices  65.5 us (34%)
  other arithmetic  29.9 us (15%)
  matrix products  28.9 us (15%)
  blocking collectives  25.5 us (13%)
  starting transfers between devices  17.1 us (9%)
  local copies, waits for them, and re-layouts  14.3 us (7%)
  between operations  13.6 us (7%)
    all_gather x1, waiting for transfers between devices, per_device(): lax.all_gather(codes, 'shard', axis=1, tiled=True)  54.4 us
    dot_general x2, matrix products, score_clusters(): jnp.dot(queries, cluster_keys.T, preferred_element_type=jnp.float32)  28.9 us
    all_gather x1, blocking collectives, per_device(): lax.all_gather(earlier_order, 'shard', axis=1, tiled=True)  25.5 us
    reduce_sum x2, other arithmetic, unit_rows(): jnp.sum(values * values, axis=-1, keepdims=True) + epsilon  21.4 us
    all_to_all x1, waiting for transfers between devices, per_device(): lax.all_to_all(send_order, 'grp', split_axis=0, concat_axis=0, tiled=True)  5.23 us
    all_to_all x1, waiting for transfers between devices, per_device(): lax.all_to_all(top_score.reshape(groups, capacity), 'grp', split_axis=0,...  5.09 us
    all_to_all x1, starting transfers between devices, per_device(): lax.all_to_all(send_order, 'grp', split_axis=0, concat_axis=0, tiled=True)  4.72 us
    all_to_all x1, starting transfers between devices, per_device(): lax.all_to_all(send_cluster, 'grp', split_axis=0, concat_axis=0, tiled=True)  4.55 us
  transfers between devices with their start and end apart: 5, of which 3 were waited for; matrix products, arithmetic and copies ran while one was open for 21% of the time, Pallas kernels for 0%

commit v1 on v0

--- a/solution.py
+++ b/solution.py
@@ -4,6 +4,13 @@
 from jax.sharding import PartitionSpec as P
 
 epsilon = 1e-06
+
+
+def swapped_in(x, mesh_axis, dim):
+    devices = lax.axis_size(mesh_axis)
+    blocks = jnp.stack([x for _ in range(devices)])
+    blocks = lax.all_to_all(blocks, mesh_axis, split_axis=0, concat_axis=0)
+    return jnp.concatenate(blocks, axis=dim)
 
 
 def unit_rows(values):
@@ -71,7 +78,7 @@
         got_rows,
         got_cluster,
         got_order,
-        lax.all_gather(codes, "shard", axis=1, tiled=True),
+        swapped_in(codes, "shard", 1),
         lax.all_gather(earlier_order, "shard", axis=1, tiled=True),
         counts,
         decode_one,

time: 195 us -> 704 us (3.61)
  blocking collectives: 25.5 us -> 568 us
  waiting for transfers between devices: 65.5 us -> 5.1 us
  other arithmetic: 29.9 us -> 55.7 us
  between operations: 13.6 us -> 0.26 us
  local copies, waits for them, and re-layouts: 14.3 us -> 23.8 us
    all_gather x1, blocking collectives: 25.5 us -> 558 us  [per_device(): lax.all_gather(earlier_order, 'shard', axis=1, tiled=True)]
    all_gather x1 -> x0, waiting for transfers between devices: 54.4 us -> none  [per_device(): lax.all_gather(codes, 'shard', axis=1, tiled=True)]
    convert_element_type x1 -> x2, other arithmetic: 1.36 us -> 28.6 us  [unit_rows(): (values / jnp.sqrt(jnp.sum(values * values, axis=-1, keepdims=True) + eps...]
    another operation x2 -> x3, local copies, waits for them, and re-layouts: 0.1 us -> 11.9 us  [the longest x1 11.8 us: swapped_in(): blocks = jnp.stack([x for _ in range(devices)])]
    all_to_all x0 -> x1, blocking collectives: none -> 9.59 us  [per_device(): lax.all_to_all(send_cluster, 'grp', split_axis=0, concat_axis=0, tiled=True)]
  transfers between devices with their start and end apart: 5 -> 4, of which waited for: 3 -> 1; matrix products, arithmetic and copies ran while one was open for 21% -> 8% of each run, Pallas kernels for 0% -> 0%
where the time goes in v1:
time: 704 us; the launch traced here: 701 us
  blocking collectives  568 us (81%)
  other arithmetic  55.7 us (8%)
  matrix products  27.3 us (4%)
  local copies, waits for them, and re-layouts  23.8 us (3%)
  starting transfers between devices  21.2 us (3%)
    all_gather x1, blocking collectives, per_device(): lax.all_gather(earlier_order, 'shard', axis=1, tiled=True)  558 us
    convert_element_type x2, other arithmetic, unit_rows(): (values / jnp.sqrt(jnp.sum(values * values, axis=-1, keepdims=True) + eps...  28.6 us
    dot_general x2, matrix products, score_clusters(): jnp.dot(queries, cluster_keys.T, preferred_element_type=jnp.float32)  27.3 us
    reduce_sum x2, other arithmetic, unit_rows(): jnp.sum(values * values, axis=-1, keepdims=True) + epsilon  20.5 us
  transfers between devices with their start and end apart: 4, of which 1 were waited for; matrix products, arithmetic and copies ran while one was open for 8% of the time, Pallas kernels for 0%

profile of v1, /device:TPU:0, one launch (start us, length us, event | category | flops | bytes accessed | tf_op | source)
XLA Modules:
  0.0 701.3 jit_solution(5184262825892293871)
XLA Ops:
  0.0 0.7 and_select_fusion
  0.7 1.2 reduce-window.6
  1.9 0.1 slice.58
  2.0 0.1 copy.15
  2.2 0.1 copy.16
  2.4 0.2 select_reduce_fusion.2
  2.5 0.2 fusion.2
  2.7 3.5 gather_fusion.2
  6.2 3.5 gather_fusion.3
  9.8 0.6 select_select_fusion.1
  10.4 9.6 %all_to_all.34 = s32[4,1,128]{2,1,0:T(1,128)S(1)} all-to-all(s32[4,1,128]{2,1,0:T(1,128)S(1)} %bitcast.69), channel_id=1, replica_groups=mesh['grp'=4,'shard'=32] {'grp'}, dimensions={0} | all-to-all | bytes 4096 | tf_op jit(solution)/shard_map/all_to_all | solution.py:63
  19.9 11.8 %stack.2 = bf16[32,2,256,1024]{3,2,1,0:T(8,128)(2,1)} broadcast(bf16[2,256,1024]{2,1,0:T(8,128)(2,1)} %param.13), dimensions={1,2,3} | broadcast | bytes 34603008 | tf_op jit(solution)/shard_map/stack | solution.py:11
  31.8 8.4 %all-to-all-start.3 = ((bf16[32,2,256,1024]{3,2,1,0:T(8,128)(2,1)}), bf16[32,2,256,1024]{3,2,1,0:T(8,128)(2,1)}, u32[]{:S(2)}, u32[]{:S(2)}) async-start(bf16[32,2,256,1024]{3,2,1,0:T(8,128)(2,1)} %stack.2), calls=%async_computation.3 | async-start | bytes 67108864 | tf_op jit(solution)/shard_map/all_to_all | solution.py:12
  40.2 0.2 fusion
  40.4 0.2 fusion.1
  40.7 2.1 gather_fusion
  42.7 558.4 %all_gather.3 = s32[2,8192]{1,0:T(2,128)S(1)} all-gather(s32[2,256]{1,0:T(2,128)S(1)} %copy-done.5), channel_id=1, replica_groups=mesh['grp'=4,'shard'=32] {'shard'}, dimensions={1}, use_global_device_ids=true | all-gather | bytes 67584 | tf_op jit(solution)/shard_map/all_gather | solution.py:82
  601.1 0.6 fusion.9
  601.7 0.7 iota_compare_fusion.2
  602.4 0.6 iota_compare_fusion.1
  603.0 1.1 broadcast_select_fusion
  604.2 3.2 all-to-all-start.1
  607.4 20.3 %multiply_reduce_fusion.1 = (f32[32,256]{1,0:T(8,128)S(1)}, f32[32,256]{1,0:T(8,128)S(1)}) fusion(f32[1024]{0:T(1024)S(1)} %bitcast.63, f32[1024]{0:T(1024)S(1)} %bitcast.59, bf16[2,32,256,1024]{3,2,0,1:T(8,128)(2,1)} %bitcast.13, f32[1024]{0:T(1024)S(1)} %bitcast.61, f32[1024]{0:T(1024)S(1)} %bitcast.57), kind=kLoop, calls=%fused_computation.8 | loop fusion | flops 83869696 | bytes 33636352 | tf_op jit(solution)/shard_map/reduce_sum | solution.py:17
  627.8 4.8 all-to-all-start.2
  632.6 28.4 %divide_convert_fusion.1 = (bf16[1,32,256,1024]{3,2,0,1:T(8,128)(2,1)}, bf16[1,32,256,1024]{3,2,0,1:T(8,128)(2,1)}) fusion(f32[32,256]{1,0:T(8,128)S(1)} %get-tuple-element.27, f32[1024]{0:T(1024)S(1)} %bitcast.64, f32[1024]{0:T(1024)S(1)} %bitcast.60, bf16[2,32,256,1024]{3,2,0,1:T(8,128)(2,1)} %bitcast.13, f32[32,256]{1,0:T(8,128)S(1)} %get-tuple-element.26, ...), kind=kLoop, calls=%fused_computation.7 | loop fusion | flops 83886080 | bytes 67190784 | tf_op jit(solution)/shard_map/convert_element_type | solution.py:17
  661.0 13.6 %select_reduce_fusion.1 = f32[512]{0:T(512)S(1)} fusion(bf16[512,1024]{1,0:T(8,128)(2,1)S(1)} %bitcast.54, bf16[8192,1024]{1,0:T(8,128)(2,1)} %bitcast.52, s32[8192]{0:T(1024)S(1)} %bitcast.66, s32[512]{0:T(512)S(1)} %bitcast.71, pred[8192]{0:T(1024)(128)(4,1)S(1)} %iota_compare_fusion.2, pred[512]{0:T(512)(128)(4,1)S(1)} %bitcast.74), kind=kOutput, calls=%fused_computation.11 | convolution fusion | flops 8610906112 | bytes 17871360 | tf_op jit(solution)/shard_map/dot_general | solution.py:30
  674.6 13.7 %select_reduce_fusion = f32[512]{0:T(512)S(1)} fusion(bf16[512,1024]{1,0:T(8,128)(2,1)S(1)} %bitcast.55, bf16[8192,1024]{1,0:T(8,128)(2,1)} %bitcast.51, s32[8192]{0:T(1024)S(1)} %bitcast.65, s32[512]{0:T(512)S(1)} %bitcast.72, pred[8192]{0:T(1024)(128)(4,1)S(1)} %iota_compare_fusion.1, pred[512]{0:T(512)(128)(4,1)S(1)} %bitcast.73), kind=kOutput, calls=%fused_computation.10 | convolution fusion | flops 8610906112 | bytes 17871360 | tf_op jit(solution)/shard_map/dot_general | solution.py:30
  688.3 0.6 maximum_maximum_fusion
  688.9 4.8 all-to-all-start.4
  693.7 5.1 all-to-all-done.4
  698.8 1.9 gather_fusion.1
  700.8 0.6 and_select_fusion.1
  (35 shorter events, 0.4 us)
Async XLA Ops:
  0.0 6.2 copy-start
  31.7 8.5 %copy-start.2 = (bf16[256,1024]{1,0:T(8,128)(2,1)S(1)}, bf16[256,1024]{1,0:T(8,128)(2,1)}, u32[]{:S(2)}) copy-start(bf16[256,1024]{1,0:T(8,128)(2,1)} %param.10) | copy-start | bytes 1572868
  31.7 11.0 %copy-start.5 = (s32[2,256]{1,0:T(2,128)S(1)}, s32[2,256]{1,0:T(2,128)}, u32[]{:S(2)}) copy-start(s32[2,256]{1,0:T(2,128)} %param.17) | copy-start | bytes 6148
  31.7 569.4 %copy-start.6 = (s32[2]{0:T(128)S(1)}, s32[2]{0:T(128)}, u32[]{:S(2)}) copy-start(s32[2]{0:T(128)} %param.16) | copy-start | bytes 28
  31.7 571.2 %copy-start.3 = (f32[2,1024]{1,0:T(2,128)S(1)}, f32[2,1024]{1,0:T(2,128)}, u32[]{:S(2)}) copy-start(f32[2,1024]{1,0:T(2,128)} %param.14) | copy-start | bytes 24580
  31.8 571.2 %copy-start.4 = (f32[2,1024]{1,0:T(2,128)S(1)}, f32[2,1024]{1,0:T(2,128)}, u32[]{:S(2)}) copy-start(f32[2,1024]{1,0:T(2,128)} %param.15) | copy-start | bytes 24580
  31.8 572.5 %all-to-all-start.3 = ((bf16[32,2,256,1024]{3,2,1,0:T(8,128)(2,1)}), bf16[32,2,256,1024]{3,2,1,0:T(8,128)(2,1)}, u32[]{:S(2)}, u32[]{:S(2)}) async-start(bf16[32,2,256,1024]{3,2,1,0:T(8,128)(2,1)} %stack.2), calls=%async_computation.3 | async-start | bytes 67108864 | tf_op jit(solution)/shard_map/all_to_all | solution.py:12
  604.2 23.5 %all-to-all-start.1 = ((s32[4,1,128]{2,1,0:T(1,128)}), s32[4,1,128]{2,1,0:T(1,128)S(1)}, u32[]{:S(2)}, u32[]{:S(2)}) async-start(s32[4,1,128]{2,1,0:T(1,128)} %bitcast.6), calls=%async_computation.1 | async-start | bytes 4096 | tf_op jit(solution)/shard_map/all_to_all | solution.py:64
  627.8 33.2 %all-to-all-start.2 = ((bf16[4,128,1024]{2,1,0:T(8,128)(2,1)}), bf16[4,128,1024]{2,1,0:T(8,128)(2,1)S(1)}, u32[]{:S(2)}, u32[]{:S(2)}) async-start(bf16[4,128,1024]{2,1,0:T(8,128)(2,1)} %broadcast_select_fusion), calls=%async_computation.2 | async-start | bytes 2097152 | tf_op jit(solution)/shard_map/all_to_all | solution.py:62
  674.6 26.7 %copy-start.1 = (s32[256]{0:T(256)S(1)}, s32[256]{0:T(256)}, u32[]{:S(2)}) copy-start(s32[256]{0:T(256)} %param.12) | copy-start | bytes 3076
  688.9 9.9 %all-to-all-start.4 = ((f32[4,1,128]{2,1,0:T(1,128)}), f32[4,1,128]{2,1,0:T(1,128)S(1)}, u32[]{:S(2)}, u32[]{:S(2)}) async-start(f32[4,1,128]{2,1,0:T(1,128)} %bitcast.22), calls=%async_computation.4 | async-start | bytes 4096 | tf_op jit(solution)/shard_map/all_to_all | solution.py:86
